TPU v7x, 768 devices: a whole 4x8x12 slice. The times are simulated.
768 devices in a mesh: ty: 16 (over x, y_lo), tx: 48 (over z, y_hi, core).
Axes of the slice: x: 4, y: 8 (y_hi: 2, y_lo: 4; y = y_hi * 4 + y_lo), z: 12, core: 2. Of those that a mesh axis runs over, the one named last changes fastest.
Arguments:
- transmission: float32 [2, 2, 1024, 3072], P(None, None, 'ty', 'tx'), may hold values from -4 to 4
- probe_field: float32 [2, 128, 128], replicated, may hold values from -4 to 4
- propagator_phase: float32 [128, 128], replicated, may hold values from -3.140625 to 3.140625
- scan_offsets: int32 [16, 48, 6, 2], P('ty', 'tx'), may hold values from 0 to 64, as said below
- position_counts: int32 [16, 48], P('ty', 'tx'), may hold values from 1 to 6, as said below
- intensities: float32 [16, 48, 6, 128, 128], P('ty', 'tx'), may hold values from 0 to 2
Outputs:
- updated_object: float32 [2, 2, 1024, 3072], P(None, None, 'ty', 'tx')
Inputs may be any that keep to these rules, and one draw needn't show every extreme that they name: `scan_offsets`: each pair is a row and a column offset within the extended region of 192 pixels; offsets 0 and 64 both occur. `position_counts`: positions k of a tile with k >= its count are ignored; some tile has 6 and some tile has 1.
All inputs are finite; a program needn't handle non-finite values.
Results may differ from a plain program's by a relative error of at most 0.0003.
Values sent between devices are 32-bit elements; how exact they have to be, the bound alone decides.
A program may use at most 32 MiB of HBM per device.

v0:
```python
import functools
import math

import jax
import jax.numpy as jnp
import numpy as np
from jax import lax
from jax.experimental import pallas as pl
from jax.experimental.pallas import tpu as pltpu
from jax.sharding import PartitionSpec as P

ITERS = 2
STEP = 0.003
SIZE = 128
CORE = 64
SLOTS = 6
F32 = jnp.float32
BF16 = jnp.bfloat16

UP, DOWN, OUT, PAIR, OUT_UP, OUT_DOWN, PAIR_UP, PAIR_DOWN = range(8)
ROW_UP, ROW_DOWN, ROW_OWN = range(3)
ROW_START = (0, 128, 64)
COL_OUT, COL_OWN, COL_PAIR = range(3)
ADD_PAIR, CORNER_UP, CORNER_DOWN, ADD_UP, ADD_DOWN, ADD_OUT = range(6)
COPIES = 14


def dft_blocks():
    index = np.arange(SIZE)
    angle = 2.0 * math.pi / SIZE * ((index[:, None] * index[None, :]) % SIZE)
    re = np.cos(angle) / math.sqrt(SIZE)
    im = -np.sin(angle) / math.sqrt(SIZE)
    right = np.block([[re, im], [-im, re]])
    blocks = np.stack([right, right.T])
    high = blocks.astype(BF16)
    low = (blocks - high.astype(np.float64)).astype(BF16)
    return np.stack([high, low], axis=1)


def split(x):
    high = x.astype(BF16)
    return high, (x - high.astype(F32)).astype(BF16)


def dot(a, b):
    return jnp.dot(a, b, preferred_element_type=F32)


def from_right(fields, table):
    high, low = split(
        jnp.concatenate(
            [
                jnp.concatenate([fields[0], fields[1]], axis=1),
                jnp.concatenate([fields[2], fields[3]], axis=1),
            ],
            axis=0,
        )
    )
    out = dot(high, table[0]) + dot(low, table[0]) + dot(high, table[1])
    return out[:SIZE, :SIZE], out[:SIZE, SIZE:], out[SIZE:, :SIZE], out[SIZE:, SIZE:]


def from_left(fields, table):
    high, low = split(
        jnp.concatenate(
            [
                jnp.concatenate([fields[0], fields[2]], axis=1),
                jnp.concatenate([fields[1], fields[3]], axis=1),
            ],
            axis=0,
        )
    )
    out = dot(table[0], high) + dot(table[0], low) + dot(table[1], high)
    return out[:SIZE, :SIZE], out[SIZE:, :SIZE], out[:SIZE, SIZE:], out[SIZE:, SIZE:]


def times(a, b):
    return a[0] * b[0] - a[1] * b[1], a[0] * b[1] + a[1] * b[0]


def times_conj(a, b):
    return a[0] * b[0] + a[1] * b[1], a[1] * b[0] - a[0] * b[1]


def lanes_of(shape):
    return lax.broadcasted_iota(jnp.int32, shape, 1)


def load_window(ext, offs, slice_, slot):
    row, col = offs[0, 0, slot, 0], offs[0, 0, slot, 1]
    rows = pl.ds(row, SIZE)
    back = lax.rem(SIZE - col, SIZE)
    keep = lanes_of((SIZE, SIZE)) < SIZE - col
    last = ext[slice_, 2, rows, :]
    re = jnp.where(
        keep, pltpu.roll(ext[slice_, 0, rows, :], back, 1), pltpu.roll(last, back, 1)
    )
    im = jnp.where(
        keep, pltpu.roll(ext[slice_, 1, rows, :], back, 1), pltpu.roll(last, CORE - col, 1)
    )
    return re, im


def store_field(padded, offs, slot, field):
    col = offs[0, 0, slot, 1]
    for part in range(2):
        padded[slot, part, CORE : CORE + SIZE, :] = pltpu.roll(field[part], col, 1)


def gradient_rows(padded, offs, start):
    lane = lanes_of((CORE, SIZE))
    sums = [jnp.zeros((CORE, SIZE), F32) for _ in range(4)]
    for slot in range(SLOTS):
        row, col = offs[0, 0, slot, 0], offs[0, 0, slot, 1]
        rows = pl.ds(CORE + start - row, CORE)
        here = lane >= col
        for part in range(2):
            value = padded[slot, part, rows, :]
            sums[part] = sums[part] + jnp.where(here, value, 0.0)
            sums[2 + part] = sums[2 + part] + jnp.where(here, 0.0, value)
    low = lane < CORE
    first = jnp.where(low, sums[0], pltpu.roll(sums[1], CORE, 1))
    second = jnp.where(low, pltpu.roll(sums[0], CORE, 1), sums[1])
    third = jnp.where(low, sums[2], pltpu.roll(sums[3], CORE, 1))
    return first, second, third


def forward_first(ext, offs, probe, prop, tables, psi):
    for pair in range(SLOTS // 2):
        fields = ()
        for slot in (2 * pair, 2 * pair + 1):
            fields += times(
                (probe[0], probe[1]), load_window(ext, offs, 0, slot)
            )
        fields = from_right(fields, tables[0])
        fields = from_left(fields, tables[1])
        factor = (prop[0], prop[1])
        fields = times(fields[:2], factor) + times(fields[2:], factor)
        fields = from_left(fields, tables[0])
        fields = from_right(fields, tables[1])
        for n in range(2):
            for part in range(2):
                psi[2 * pair + n, part] = fields[2 * n + part]


def middle(ext, offs, counts, measured, tables, psi, back, padded):
    for pair in range(SLOTS // 2):
        slots = (2 * pair, 2 * pair + 1)
        windows, fields = [], ()
        for slot in slots:
            window = load_window(ext, offs, 1, slot)
            windows.append(window)
            fields += times((psi[slot, 0], psi[slot, 1]), window)
        fields = from_right(fields, tables[0])
        fields = from_left(fields, tables[1])
        grads = ()
        for n, slot in enumerate(slots):
            re, im = fields[2 * n], fields[2 * n + 1]
            live = jnp.where(slot < counts[0, 0], 4.0, 0.0)
            factor = live * (re * re + im * im - measured[0, 0, slot])
            grads += (factor * re, factor * im)
        grads = from_left(grads, tables[0])
        grads = from_right(grads, tables[1])
        for n, slot in enumerate(slots):
            grad = grads[2 * n : 2 * n + 2]
            field = times_conj(grad, windows[n])
            for part in range(2):
                back[slot, part] = field[part]
            store_field(
                padded, offs, slot, times_conj(grad, (psi[slot, 0], psi[slot, 1]))
            )


def backward_first(offs, probe, prop, tables, back, padded):
    for pair in range(SLOTS // 2):
        slots = (2 * pair, 2 * pair + 1)
        fields = ()
        for slot in slots:
            fields += (back[slot, 0], back[slot, 1])
        fields = from_right(fields, tables[0])
        fields = from_left(fields, tables[1])
        factor = (prop[0], prop[1])
        fields = times_conj(fields[:2], factor) + times_conj(fields[2:], factor)
        fields = from_left(fields, tables[0])
        fields = from_right(fields, tables[1])
        for n, slot in enumerate(slots):
            store_field(
                padded,
                offs,
                slot,
                times_conj(fields[2 * n : 2 * n + 2], (probe[0], probe[1])),
            )


def kernel(
    mesh_shape,
    obj,
    probe,
    phase,
    offs,
    counts,
    measured,
    tables,
    out,
    own,
    halo,
    grads,
    passed,
    added,
    ext,
    prop,
    psi,
    back,
    padded,
    send_sems,
    recv_sems,
):
    ty_count, tx_count = mesh_shape
    row, col = lax.axis_index("ty"), lax.axis_index("tx")
    even = lax.rem(col, 2) == 0
    above = {"ty": lax.rem(row + ty_count - 1, ty_count)}
    below = {"ty": lax.rem(row + 1, ty_count)}
    right = lax.rem(col + 1, tx_count)
    left = lax.rem(col + tx_count - 1, tx_count)
    outer = {"tx": jnp.where(even, left, right)}
    partner = {"tx": jnp.where(even, right, left)}
    has_above = row > 0
    has_below = row < ty_count - 1
    has_outer = jnp.logical_and(col > 0, col < tx_count - 1)

    barrier = pltpu.get_barrier_semaphore()
    for target in (above, below, outer, partner):
        pl.semaphore_signal(
            barrier, inc=1, device_id=target, device_id_type=pl.DeviceIdType.MESH
        )

    low = lanes_of((CORE, SIZE)) < CORE
    for s in range(2):
        re = jnp.concatenate([obj[0, s], obj[1, s]], axis=1)
        own[0, s] = re
    pl.semaphore_wait(barrier, 4)

    started = []

    def send(src, dst, step, s, kind, target):
        copy = pltpu.make_async_remote_copy(
            src_ref=src,
            dst_ref=dst,
            send_sem=send_sems.at[step, s, kind],
            recv_sem=recv_sems.at[step, s, kind],
            device_id=target,
            device_id_type=pl.DeviceIdType.MESH,
        )
        copy.start()
        started.append(copy)
        return copy

    def send_halo(step, s, kind, src, target):
        return send(src, halo.at[step, s, kind], step, s, kind, target)

    def halo_first(step, s):
        mine = own.at[step, s]
        return {
            OUT: send_halo(step, s, OUT, mine, outer),
            DOWN: send_halo(step, s, DOWN, mine, above),
            UP: send_halo(step, s, UP, mine, below),
            PAIR: send_halo(step, s, PAIR, mine, partner),
        }

    def halo_second(step, s, copies):
        copies[OUT].wait_recv()
        copies[OUT_DOWN] = send_halo(step, s, OUT_DOWN, halo.at[step, s, OUT], above)
        copies[OUT_UP] = send_halo(step, s, OUT_UP, halo.at[step, s, OUT], below)
        copies[UP].wait_recv()
        copies[PAIR_UP] = send_halo(step, s, PAIR_UP, halo.at[step, s, UP], partner)
        copies[DOWN].wait_recv()
        copies[PAIR_DOWN] = send_halo(
            step, s, PAIR_DOWN, halo.at[step, s, DOWN], partner
        )

    def place(s, start, out_tile, own_tile, pair_tile):
        first = jnp.where(even, out_tile, pair_tile)
        third = jnp.where(even, pair_tile, out_tile)
        rows = slice(start, start + CORE)
        ext[s, 0, rows, :] = jnp.where(low, first, pltpu.roll(own_tile, CORE, 1))
        ext[s, 1, rows, :] = jnp.where(low, pltpu.roll(first, CORE, 1), own_tile)
        ext[s, 2, rows, :] = third

    def halo_last(step, s, copies):
        for kind in (PAIR, OUT_UP, PAIR_UP, OUT_DOWN, PAIR_DOWN):
            copies[kind].wait_recv()
        tile = lambda kind, ok: jnp.where(ok, halo[step, s, kind], 0.0)
        both = jnp.logical_and
        place(s, CORE, tile(OUT, has_outer), own[step, s], halo[step, s, PAIR])
        place(
            s,
            0,
            tile(OUT_UP, both(has_outer, has_above)),
            tile(UP, has_above),
            tile(PAIR_UP, has_above),
        )
        place(
            s,
            2 * CORE,
            tile(OUT_DOWN, both(has_outer, has_below)),
            tile(DOWN, has_below),
            tile(PAIR_DOWN, has_below),
        )

    def reduce_first(step, s):
        for tile in (ROW_UP, ROW_DOWN, ROW_OWN):
            first, second, third = gradient_rows(padded.at[s], offs, ROW_START[tile])
            grads[step, s, COL_PAIR, tile] = jnp.where(even, third, first)
            grads[step, s, COL_OUT, tile] = jnp.where(even, first, third)
            grads[step, s, COL_OWN, tile] = second
        sent = grads.at[step, s]
        return {
            CORNER_DOWN: send(
                sent.at[COL_OUT, ROW_UP],
                added.at[step, s, CORNER_DOWN - 1],
                step,
                s,
                8 + CORNER_DOWN,
                above,
            ),
            CORNER_UP: send(
                sent.at[COL_OUT, ROW_DOWN],
                added.at[step, s, CORNER_UP - 1],
                step,
                s,
                8 + CORNER_UP,
                below,
            ),
            ADD_PAIR: send(
                sent.at[COL_PAIR], passed.at[step, s], step, s, 8 + ADD_PAIR, partner
            ),
        }

    def masked(step, s, kind, ok):
        return jnp.where(ok, added[step, s, kind - 1], 0.0)

    def reduce_second(step, s, copies):
        mine = grads.at[step, s]

        def pass_on(kind, src, target):
            copies[kind] = send(
                src, added.at[step, s, kind - 1], step, s, 8 + kind, target
            )

        copies[ADD_PAIR].wait_recv()
        for tile, kind, target in ((ROW_UP, ADD_DOWN, above), (ROW_DOWN, ADD_UP, below)):
            mine[COL_OWN, tile] = mine[COL_OWN, tile] + passed[step, s, tile]
            pass_on(kind, mine.at[COL_OWN, tile], target)
        copies[CORNER_UP].wait_recv()
        copies[CORNER_DOWN].wait_recv()
        mine[COL_OUT, ROW_OWN] = (
            mine[COL_OUT, ROW_OWN]
            + masked(step, s, CORNER_UP, has_above)
            + masked(step, s, CORNER_DOWN, has_below)
        )
        pass_on(ADD_OUT, mine.at[COL_OUT, ROW_OWN], outer)

    def reduce_last(step, s, copies):
        total = grads[step, s, COL_OWN, ROW_OWN] + passed[step, s, ROW_OWN]
        for kind, ok in ((ADD_UP, has_above), (ADD_DOWN, has_below), (ADD_OUT, has_outer)):
            copies[kind].wait_recv()
            total = total + masked(step, s, kind, ok)
        return own[step, s] - STEP * total

    first0 = halo_first(0, 0)
    first1 = halo_first(0, 1)
    prop[0] = jnp.cos(phase[...])
    prop[1] = jnp.sin(phase[...])
    zero = jnp.zeros((CORE, SIZE), F32)
    for s in range(2):
        for slot in range(SLOTS):
            for part in range(2):
                padded[s, slot, part, :CORE, :] = zero
                padded[s, slot, part, CORE + SIZE :, :] = zero

    for step in range(ITERS):
        halo_second(step, 0, first0)
        halo_second(step, 1, first1)
        halo_last(step, 0, first0)
        forward_first(ext, offs, probe, prop, tables, psi)
        halo_last(step, 1, first1)
        middle(ext, offs, counts, measured, tables, psi, back, padded.at[1])
        sums1 = reduce_first(step, 1)
        backward_first(offs, probe, prop, tables, back, padded.at[0])
        reduce_second(step, 1, sums1)
        sums0 = reduce_first(step, 0)
        reduce_second(step, 0, sums0)
        for s, sums in ((0, sums0), (1, sums1)):
            new = reduce_last(step, s, sums)
            if step < ITERS - 1:
                own[step + 1, s] = new
                copies = halo_first(step + 1, s)
                if s == 0:
                    first0 = copies
                else:
                    first1 = copies
            else:
                out[0, s] = new[:, :CORE]
                out[1, s] = pltpu.roll(new, CORE, 1)[:, :CORE]
    for copy in started:
        copy.wait_send()


def solution(mesh):
    shape = (mesh.shape["ty"], mesh.shape["tx"])
    vmem = pl.BlockSpec(memory_space=pltpu.VMEM)
    smem = pl.BlockSpec(memory_space=pltpu.SMEM)
    tables = dft_blocks()

    def on_device(
        transmission, probe_field, propagator_phase, scan_offsets, position_counts, intensities
    ):
        tile = (CORE, SIZE)
        field = (SIZE, SIZE)
        return pl.pallas_call(
            functools.partial(kernel, shape),
            out_shape=jax.ShapeDtypeStruct(transmission.shape, F32),
            in_specs=[vmem, vmem, vmem, smem, smem, vmem, vmem],
            out_specs=vmem,
            scratch_shapes=[
                pltpu.VMEM((ITERS, 2) + tile, F32),
                pltpu.VMEM((ITERS, 2, 8) + tile, F32),
                pltpu.VMEM((ITERS, 2, 3, 3) + tile, F32),
                pltpu.VMEM((ITERS, 2, 3) + tile, F32),
                pltpu.VMEM((ITERS, 2, 5) + tile, F32),
                pltpu.VMEM((2, 3, 3 * CORE, SIZE), F32),
                pltpu.VMEM((2,) + field, F32),
                pltpu.VMEM((SLOTS, 2) + field, F32),
                pltpu.VMEM((SLOTS, 2) + field, F32),
                pltpu.VMEM((2, SLOTS, 2, 2 * SIZE, SIZE), F32),
                pltpu.SemaphoreType.DMA((ITERS, 2, COPIES)),
                pltpu.SemaphoreType.DMA((ITERS, 2, COPIES)),
            ],
            compiler_params=pltpu.CompilerParams(
                collective_id=0, has_side_effects=True, vmem_limit_bytes=48 * 1024 * 1024
            ),
        )(
            transmission,
            probe_field,
            propagator_phase,
            scan_offsets,
            position_counts,
            intensities,
            jnp.asarray(tables),
        )

    return jax.shard_map(
        on_device,
        mesh=mesh,
        in_specs=(
            P(None, None, "ty", "tx"),
            P(),
            P(),
            P("ty", "tx", None, None),
            P("ty", "tx"),
            P("ty", "tx", None, None, None),
        ),
        out_specs=P(None, None, "ty", "tx"),
        check_vma=False,
    )
```

profile of v0, /device:TPU:1, one launch (start us, length us, event | category | flops | bytes accessed | tf_op | source)
XLA Modules:
  0.0 89.5 jit_solution(1311621962134379)
XLA Ops:
  0.0 0.0 copy-start.5
  0.7 0.0 copy-done.5
  0.7 0.1 copy.8.offs
  0.8 0.0 copy-start
  0.8 1.0 %copy-done = bf16[2,2,256,256]{3,2,1,0:T(8,128)(2,1)S(1)} copy-done((bf16[2,2,256,256]{3,2,1,0:T(8,128)(2,1)S(1)}, bf16[2,2,256,256]{3,2,1,0:T(8,128)(2,1)}, u32[]{:S(2)}) %copy-start) | copy-done | bytes 524312
  1.8 0.0 copy-start.1
  1.8 1.0 %copy-done.1 = f32[1,1,6,128,128]{4,3,2,1,0:T(8,128)S(1)} copy-done((f32[1,1,6,128,128]{4,3,2,1,0:T(8,128)S(1)}, f32[1,1,6,128,128]{4,3,2,1,0:T(8,128)}, u32[]{:S(2)}) %copy-start.1) | copy-done | bytes 393240
  2.8 0.0 copy-start.2
  2.8 0.9 %copy-done.2 = f32[2,2,64,64]{3,2,1,0:T(8,128)S(1)} copy-done((f32[2,2,64,64]{3,2,1,0:T(8,128)S(1)}, f32[2,2,64,64]{3,2,1,0:T(8,128)}, u32[]{:S(2)}) %copy-start.2) | copy-done | bytes 65560
  3.7 0.0 copy-start.3
  3.7 0.9 %copy-done.3 = f32[2,128,128]{2,1,0:T(8,128)S(1)} copy-done((f32[2,128,128]{2,1,0:T(8,128)S(1)}, f32[2,128,128]{2,1,0:T(8,128)}, u32[]{:S(2)}) %copy-start.3) | copy-done | bytes 131096
  4.6 0.0 copy-start.4
  4.6 0.8 copy-done.4
  5.5 83.4 %shard_map.73 = f32[2,2,64,64]{3,2,1,0:T(8,128)S(1)} custom-call(f32[2,2,64,64]{3,2,1,0:T(8,128)S(1)} %copy-done.2, f32[2,128,128]{2,1,0:T(8,128)S(1)} %copy-done.3, f32[128,128]{1,0:T(8,128)S(1)} %copy-done.4, s32[1,1,6,2]{3,2,1,0:T(8,128)S(1)} %copy.8.offs, s32[1,1]{1,0:T(1,128)S(6)} %copy.10.counts, f32[1,1,6,128,128]{4,3,2,1,0:T(8,128)S(1)} %copy-done.1, ...), custom_call_target="tpu_custom_call" | custom-call | tf_op jit(solution)/shard_map/pallas_call | solution.py:420
  88.9 0.7 copy.11
Async XLA Ops:
  0.0 0.7 copy-start.5
  0.8 1.0 %copy-start = (bf16[2,2,256,256]{3,2,1,0:T(8,128)(2,1)S(1)}, bf16[2,2,256,256]{3,2,1,0:T(8,128)(2,1)}, u32[]{:S(2)}) copy-start(bf16[2,2,256,256]{3,2,1,0:T(8,128)(2,1)} %constant.2.clone.tables) | copy-start | bytes 1572868
  1.8 1.0 %copy-start.1 = (f32[1,1,6,128,128]{4,3,2,1,0:T(8,128)S(1)}, f32[1,1,6,128,128]{4,3,2,1,0:T(8,128)}, u32[]{:S(2)}) copy-start(f32[1,1,6,128,128]{4,3,2,1,0:T(8,128)} %measured.1) | copy-start | bytes 1179652
  2.8 0.9 %copy-start.2 = (f32[2,2,64,64]{3,2,1,0:T(8,128)S(1)}, f32[2,2,64,64]{3,2,1,0:T(8,128)}, u32[]{:S(2)}) copy-start(f32[2,2,64,64]{3,2,1,0:T(8,128)} %obj.1) | copy-start | bytes 196612
  3.7 0.9 %copy-start.3 = (f32[2,128,128]{2,1,0:T(8,128)S(1)}, f32[2,128,128]{2,1,0:T(8,128)}, u32[]{:S(2)}) copy-start(f32[2,128,128]{2,1,0:T(8,128)} %probe.1) | copy-start | bytes 393220
  4.6 0.8 copy-start.4
where the time goes:
time: 89.8 us; the launch traced here: 89.5 us
  Pallas kernels  83.4 us (93%)
  local copies, waits for them, and re-layouts  5.45 us (6%)
    pallas_call x1, Pallas kernels, on_device(): pl.pallas_call(functools.partial(kernel, shape), out_shape=jax.ShapeDtype...  83.4 us
    unnamed x14, local copies, waits for them, and re-layouts  5.45 us

commit v1 on v0

--- a/solution.py
+++ b/solution.py
@@ -87,7 +87,7 @@
 
 
 def load_window(ext, offs, slice_, slot):
-    row, col = offs[0, 0, slot, 0], offs[0, 0, slot, 1]
+    row, col = offs[0, 0, 0, slot], offs[0, 0, 1, slot]
     rows = pl.ds(row, SIZE)
     back = lax.rem(SIZE - col, SIZE)
     keep = lanes_of((SIZE, SIZE)) < SIZE - col
@@ -102,7 +102,7 @@
 
 
 def store_field(padded, offs, slot, field):
-    col = offs[0, 0, slot, 1]
+    col = offs[0, 0, 1, slot]
     for part in range(2):
         padded[slot, part, CORE : CORE + SIZE, :] = pltpu.roll(field[part], col, 1)
 
@@ -111,7 +111,7 @@
     lane = lanes_of((CORE, SIZE))
     sums = [jnp.zeros((CORE, SIZE), F32) for _ in range(4)]
     for slot in range(SLOTS):
-        row, col = offs[0, 0, slot, 0], offs[0, 0, slot, 1]
+        row, col = offs[0, 0, 0, slot], offs[0, 0, 1, slot]
         rows = pl.ds(CORE + start - row, CORE)
         here = lane >= col
         for part in range(2):
@@ -194,6 +194,14 @@
 
 def kernel(
     mesh_shape,
+    obj_in,
+    probe_in,
+    phase_in,
+    offs_in,
+    counts_in,
+    measured_in,
+    tables_in,
+    out,
     obj,
     probe,
     phase,
@@ -201,7 +209,6 @@
     counts,
     measured,
     tables,
-    out,
     own,
     halo,
     grads,
@@ -214,31 +221,52 @@
     padded,
     send_sems,
     recv_sems,
+    load_sems,
 ):
     ty_count, tx_count = mesh_shape
     row, col = lax.axis_index("ty"), lax.axis_index("tx")
     even = lax.rem(col, 2) == 0
-    above = {"ty": lax.rem(row + ty_count - 1, ty_count)}
-    below = {"ty": lax.rem(row + 1, ty_count)}
+    up = lax.rem(row + ty_count - 1, ty_count)
+    down = lax.rem(row + 1, ty_count)
     right = lax.rem(col + 1, tx_count)
     left = lax.rem(col + tx_count - 1, tx_count)
-    outer = {"tx": jnp.where(even, left, right)}
-    partner = {"tx": jnp.where(even, right, left)}
+    side = jnp.where(even, left, right)
+    outer = {"ty": row, "tx": side}
+    partner = {"ty": row, "tx": jnp.where(even, right, left)}
+    above, below = {"ty": up, "tx": col}, {"ty": down, "tx": col}
+    outer_above, outer_below = {"ty": up, "tx": side}, {"ty": down, "tx": side}
     has_above = row > 0
     has_below = row < ty_count - 1
     has_outer = jnp.logical_and(col > 0, col < tx_count - 1)
 
     barrier = pltpu.get_barrier_semaphore()
-    for target in (above, below, outer, partner):
+    for target in (outer, outer_above, outer_below, above, below, partner):
         pl.semaphore_signal(
             barrier, inc=1, device_id=target, device_id_type=pl.DeviceIdType.MESH
         )
 
+    loads = [
+        pltpu.make_async_copy(src, dst, load_sems.at[n])
+        for n, (src, dst) in enumerate(
+            (
+                (obj_in, obj),
+                (phase_in, phase),
+                (offs_in, offs),
+                (counts_in, counts),
+                (probe_in, probe),
+                (tables_in, tables),
+                (measured_in, measured),
+            )
+        )
+    ]
+    for load in loads:
+        load.start()
+
     low = lanes_of((CORE, SIZE)) < CORE
+    loads[0].wait()
     for s in range(2):
-        re = jnp.concatenate([obj[0, s], obj[1, s]], axis=1)
-        own[0, s] = re
-    pl.semaphore_wait(barrier, 4)
+        own[0, s] = jnp.concatenate([obj[0, s], obj[1, s]], axis=1)
+    pl.semaphore_wait(barrier, 6)
 
     started = []
 
@@ -261,22 +289,23 @@
     def halo_first(step, s):
         mine = own.at[step, s]
         return {
-            OUT: send_halo(step, s, OUT, mine, outer),
-            DOWN: send_halo(step, s, DOWN, mine, above),
-            UP: send_halo(step, s, UP, mine, below),
-            PAIR: send_halo(step, s, PAIR, mine, partner),
+            kind: send_halo(step, s, kind, mine, target)
+            for kind, target in (
+                (OUT, outer),
+                (OUT_DOWN, outer_above),
+                (OUT_UP, outer_below),
+                (DOWN, above),
+                (UP, below),
+                (PAIR, partner),
+            )
         }
 
     def halo_second(step, s, copies):
-        copies[OUT].wait_recv()
-        copies[OUT_DOWN] = send_halo(step, s, OUT_DOWN, halo.at[step, s, OUT], above)
-        copies[OUT_UP] = send_halo(step, s, OUT_UP, halo.at[step, s, OUT], below)
-        copies[UP].wait_recv()
-        copies[PAIR_UP] = send_halo(step, s, PAIR_UP, halo.at[step, s, UP], partner)
-        copies[DOWN].wait_recv()
-        copies[PAIR_DOWN] = send_halo(
-            step, s, PAIR_DOWN, halo.at[step, s, DOWN], partner
-        )
+        for kind, passed_on in ((UP, PAIR_UP), (DOWN, PAIR_DOWN)):
+            copies[kind].wait_recv()
+            copies[passed_on] = send_halo(
+                step, s, passed_on, halo.at[step, s, kind], partner
+            )
 
     def place(s, start, out_tile, own_tile, pair_tile):
         first = jnp.where(even, out_tile, pair_tile)
@@ -287,7 +316,7 @@
         ext[s, 2, rows, :] = third
 
     def halo_last(step, s, copies):
-        for kind in (PAIR, OUT_UP, PAIR_UP, OUT_DOWN, PAIR_DOWN):
+        for kind in (PAIR, PAIR_UP, PAIR_DOWN, OUT_UP, OUT_DOWN, OUT):
             copies[kind].wait_recv()
         tile = lambda kind, ok: jnp.where(ok, halo[step, s, kind], 0.0)
         both = jnp.logical_and
@@ -308,67 +337,64 @@
         )
 
     def reduce_first(step, s):
-        for tile in (ROW_UP, ROW_DOWN, ROW_OWN):
+        sent = grads.at[step, s]
+        copies = {}
+        for tile, kind, target in (
+            (ROW_UP, CORNER_DOWN, outer_above),
+            (ROW_DOWN, CORNER_UP, outer_below),
+            (ROW_OWN, ADD_OUT, outer),
+        ):
             first, second, third = gradient_rows(padded.at[s], offs, ROW_START[tile])
-            grads[step, s, COL_PAIR, tile] = jnp.where(even, third, first)
-            grads[step, s, COL_OUT, tile] = jnp.where(even, first, third)
-            grads[step, s, COL_OWN, tile] = second
-        sent = grads.at[step, s]
-        return {
-            CORNER_DOWN: send(
-                sent.at[COL_OUT, ROW_UP],
-                added.at[step, s, CORNER_DOWN - 1],
+            sent[COL_OUT, tile] = jnp.where(even, first, third)
+            copies[kind] = send(
+                sent.at[COL_OUT, tile],
+                added.at[step, s, kind - 1],
                 step,
                 s,
-                8 + CORNER_DOWN,
-                above,
-            ),
-            CORNER_UP: send(
-                sent.at[COL_OUT, ROW_DOWN],
-                added.at[step, s, CORNER_UP - 1],
-                step,
-                s,
-                8 + CORNER_UP,
-                below,
-            ),
-            ADD_PAIR: send(
-                sent.at[COL_PAIR], passed.at[step, s], step, s, 8 + ADD_PAIR, partner
-            ),
-        }
+                8 + kind,
+                target,
+            )
+            sent[COL_PAIR, tile] = jnp.where(even, third, first)
+            sent[COL_OWN, tile] = second
+        copies[ADD_PAIR] = send(
+            sent.at[COL_PAIR], passed.at[step, s], step, s, 8 + ADD_PAIR, partner
+        )
+        return copies
 
     def masked(step, s, kind, ok):
         return jnp.where(ok, added[step, s, kind - 1], 0.0)
 
     def reduce_second(step, s, copies):
         mine = grads.at[step, s]
-
-        def pass_on(kind, src, target):
-            copies[kind] = send(
-                src, added.at[step, s, kind - 1], step, s, 8 + kind, target
-            )
-
         copies[ADD_PAIR].wait_recv()
         for tile, kind, target in ((ROW_UP, ADD_DOWN, above), (ROW_DOWN, ADD_UP, below)):
             mine[COL_OWN, tile] = mine[COL_OWN, tile] + passed[step, s, tile]
-            pass_on(kind, mine.at[COL_OWN, tile], target)
-        copies[CORNER_UP].wait_recv()
-        copies[CORNER_DOWN].wait_recv()
-        mine[COL_OUT, ROW_OWN] = (
-            mine[COL_OUT, ROW_OWN]
-            + masked(step, s, CORNER_UP, has_above)
-            + masked(step, s, CORNER_DOWN, has_below)
-        )
-        pass_on(ADD_OUT, mine.at[COL_OUT, ROW_OWN], outer)
+            copies[kind] = send(
+                mine.at[COL_OWN, tile],
+                added.at[step, s, kind - 1],
+                step,
+                s,
+                8 + kind,
+                target,
+            )
 
     def reduce_last(step, s, copies):
         total = grads[step, s, COL_OWN, ROW_OWN] + passed[step, s, ROW_OWN]
-        for kind, ok in ((ADD_UP, has_above), (ADD_DOWN, has_below), (ADD_OUT, has_outer)):
+        both = jnp.logical_and
+        for kind, ok in (
+            (ADD_UP, has_above),
+            (ADD_DOWN, has_below),
+            (CORNER_UP, both(has_above, has_outer)),
+            (CORNER_DOWN, both(has_below, has_outer)),
+            (ADD_OUT, has_outer),
+        ):
             copies[kind].wait_recv()
             total = total + masked(step, s, kind, ok)
         return own[step, s] - STEP * total
 
     first0 = halo_first(0, 0)
     first1 = halo_first(0, 1)
+    loads[1].wait()
     prop[0] = jnp.cos(phase[...])
     prop[1] = jnp.sin(phase[...])
     zero = jnp.zeros((CORE, SIZE), F32)
@@ -377,6 +403,9 @@
             for part in range(2):
                 padded[s, slot, part, :CORE, :] = zero
                 padded[s, slot, part, CORE + SIZE :, :] = zero
+
+    for load in loads[2:]:
+        load.wait()
 
     for step in range(ITERS):
         halo_second(step, 0, first0)
@@ -409,7 +438,7 @@
 def solution(mesh):
     shape = (mesh.shape["ty"], mesh.shape["tx"])
     vmem = pl.BlockSpec(memory_space=pltpu.VMEM)
-    smem = pl.BlockSpec(memory_space=pltpu.SMEM)
+    hbm = pl.BlockSpec(memory_space=pl.ANY)
     tables = dft_blocks()
 
     def on_device(
@@ -420,9 +449,16 @@
         return pl.pallas_call(
             functools.partial(kernel, shape),
             out_shape=jax.ShapeDtypeStruct(transmission.shape, F32),
-            in_specs=[vmem, vmem, vmem, smem, smem, vmem, vmem],
+            in_specs=[hbm] * 7,
             out_specs=vmem,
             scratch_shapes=[
+                pltpu.VMEM(transmission.shape, F32),
+                pltpu.VMEM((2,) + field, F32),
+                pltpu.VMEM(field, F32),
+                pltpu.SMEM((1, 1, 2, SLOTS), jnp.int32),
+                pltpu.SMEM((1, 1), jnp.int32),
+                pltpu.VMEM(intensities.shape, F32),
+                pltpu.VMEM(tables.shape, BF16),
                 pltpu.VMEM((ITERS, 2) + tile, F32),
                 pltpu.VMEM((ITERS, 2, 8) + tile, F32),
                 pltpu.VMEM((ITERS, 2, 3, 3) + tile, F32),
@@ -435,15 +471,16 @@
                 pltpu.VMEM((2, SLOTS, 2, 2 * SIZE, SIZE), F32),
                 pltpu.SemaphoreType.DMA((ITERS, 2, COPIES)),
                 pltpu.SemaphoreType.DMA((ITERS, 2, COPIES)),
+                pltpu.SemaphoreType.DMA((7,)),
             ],
             compiler_params=pltpu.CompilerParams(
-                collective_id=0, has_side_effects=True, vmem_limit_bytes=48 * 1024 * 1024
+                collective_id=0, has_side_effects=True, vmem_limit_bytes=60 * 1024 * 1024
             ),
         )(
             transmission,
             probe_field,
             propagator_phase,
-            scan_offsets,
+            jnp.swapaxes(scan_offsets, 2, 3),
             position_counts,
             intensities,
             jnp.asarray(tables),

time: 89.8 us -> 77.7 us (0.87)
  the two profiles are of different devices: /device:TPU:1 before, /device:TPU:8 now
where the time goes in v1:
time: 77.7 us; the launch traced here: 77.5 us
  Pallas kernels  75.3 us (97%)
  local copies, waits for them, and re-layouts  1.57 us (2%)
    pallas_call x1, Pallas kernels, on_device(): pl.pallas_call(functools.partial(kernel, shape), out_shape=jax.ShapeDtype...  75.3 us
    unnamed x1, local copies, waits for them, and re-layouts  1.57 us

profile of v1, /device:TPU:8, one launch (start us, length us, event | category | flops | bytes accessed | tf_op | source)
XLA Modules:
  0.0 77.5 jit_solution(5485769172838966552)
XLA Ops:
  0.7 75.3 %shard_map.73 = f32[2,2,64,64]{3,2,1,0:T(8,128)} custom-call(f32[2,2,64,64]{3,2,1,0:T(8,128)} %obj_in.1, f32[2,128,128]{2,1,0:T(8,128)} %probe_in.1, f32[128,128]{1,0:T(8,128)} %phase_in.1, s32[1,1,2,6]{3,2,1,0:T(2,128)} %bitcast.1, s32[1,1]{1,0:T(1,128)S(6)} %copy.9.counts_in, f32[1,1,6,128,128]{4,3,2,1,0:T(8,128)} %measured_in.1, ...), custom_call_target="tpu_custom_call" | custom-call | tf_op jit(solution)/shard_map/pallas_call | solution.py:449
  76.0 1.6 %copy.10 = f32[2,2,64,64]{3,2,1,0:T(8,128)} copy(f32[2,2,64,64]{3,2,1,0:T(8,128)} %shard_map.73) | data formatting | bytes 131072

commit v2 on v1

--- a/solution.py
+++ b/solution.py
@@ -125,45 +125,58 @@
     return first, second, third
 
 
+def transform(fields, tables, which, left_first=False):
+    order = (from_left, from_right) if left_first else (from_right, from_left)
+    for apply in order:
+        fields = [apply(field, tables[which[0]] if apply is from_right else tables[which[1]]) for field in fields]
+    return fields
+
+
+FORWARD, INVERSE = (0, 1), (1, 0)
+PAIRS = tuple((2 * pair, 2 * pair + 1) for pair in range(SLOTS // 2))
+
+
 def forward_first(ext, offs, probe, prop, tables, psi):
-    for pair in range(SLOTS // 2):
-        fields = ()
-        for slot in (2 * pair, 2 * pair + 1):
-            fields += times(
-                (probe[0], probe[1]), load_window(ext, offs, 0, slot)
-            )
-        fields = from_right(fields, tables[0])
-        fields = from_left(fields, tables[1])
-        factor = (prop[0], prop[1])
-        fields = times(fields[:2], factor) + times(fields[2:], factor)
-        fields = from_left(fields, tables[0])
-        fields = from_right(fields, tables[1])
-        for n in range(2):
+    light = (probe[0], probe[1])
+    fields = [
+        times(light, load_window(ext, offs, 0, a)) + times(light, load_window(ext, offs, 0, b))
+        for a, b in PAIRS
+    ]
+    fields = transform(fields, tables, FORWARD)
+    factor = (prop[0], prop[1])
+    fields = [times(field[:2], factor) + times(field[2:], factor) for field in fields]
+    fields = transform(fields, tables, INVERSE, True)
+    for slots, field in zip(PAIRS, fields):
+        for n, slot in enumerate(slots):
             for part in range(2):
-                psi[2 * pair + n, part] = fields[2 * n + part]
-
-
-def middle(ext, offs, counts, measured, tables, psi, back, padded):
-    for pair in range(SLOTS // 2):
-        slots = (2 * pair, 2 * pair + 1)
-        windows, fields = [], ()
+                psi[slot, part] = field[2 * n + part]
+
+
+def middle(ext, offs, counts, measured, tables, psi, back, wins, padded):
+    fields = []
+    for slots in PAIRS:
+        field = ()
         for slot in slots:
             window = load_window(ext, offs, 1, slot)
-            windows.append(window)
-            fields += times((psi[slot, 0], psi[slot, 1]), window)
-        fields = from_right(fields, tables[0])
-        fields = from_left(fields, tables[1])
-        grads = ()
+            wins[slot, 0] = window[0]
+            wins[slot, 1] = window[1]
+            field += times((psi[slot, 0], psi[slot, 1]), window)
+        fields.append(field)
+    fields = transform(fields, tables, FORWARD)
+    grads = []
+    for slots, field in zip(PAIRS, fields):
+        grad = ()
         for n, slot in enumerate(slots):
-            re, im = fields[2 * n], fields[2 * n + 1]
+            re, im = field[2 * n], field[2 * n + 1]
             live = jnp.where(slot < counts[0, 0], 4.0, 0.0)
             factor = live * (re * re + im * im - measured[0, 0, slot])
-            grads += (factor * re, factor * im)
-        grads = from_left(grads, tables[0])
-        grads = from_right(grads, tables[1])
+            grad += (factor * re, factor * im)
+        grads.append(grad)
+    grads = transform(grads, tables, INVERSE, True)
+    for slots, both in zip(PAIRS, grads):
         for n, slot in enumerate(slots):
-            grad = grads[2 * n : 2 * n + 2]
-            field = times_conj(grad, windows[n])
+            grad = both[2 * n : 2 * n + 2]
+            field = times_conj(grad, (wins[slot, 0], wins[slot, 1]))
             for part in range(2):
                 back[slot, part] = field[part]
             store_field(
@@ -172,23 +185,18 @@
 
 
 def backward_first(offs, probe, prop, tables, back, padded):
-    for pair in range(SLOTS // 2):
-        slots = (2 * pair, 2 * pair + 1)
-        fields = ()
-        for slot in slots:
-            fields += (back[slot, 0], back[slot, 1])
-        fields = from_right(fields, tables[0])
-        fields = from_left(fields, tables[1])
-        factor = (prop[0], prop[1])
-        fields = times_conj(fields[:2], factor) + times_conj(fields[2:], factor)
-        fields = from_left(fields, tables[0])
-        fields = from_right(fields, tables[1])
+    fields = [
+        (back[a, 0], back[a, 1], back[b, 0], back[b, 1]) for a, b in PAIRS
+    ]
+    fields = transform(fields, tables, FORWARD)
+    factor = (prop[0], prop[1])
+    fields = [times_conj(field[:2], factor) + times_conj(field[2:], factor) for field in fields]
+    fields = transform(fields, tables, INVERSE, True)
+    light = (probe[0], probe[1])
+    for slots, field in zip(PAIRS, fields):
         for n, slot in enumerate(slots):
             store_field(
-                padded,
-                offs,
-                slot,
-                times_conj(fields[2 * n : 2 * n + 2], (probe[0], probe[1])),
+                padded, offs, slot, times_conj(field[2 * n : 2 * n + 2], light)
             )
 
 
@@ -218,6 +226,7 @@
     prop,
     psi,
     back,
+    wins,
     padded,
     send_sems,
     recv_sems,
@@ -413,7 +422,7 @@
         halo_last(step, 0, first0)
         forward_first(ext, offs, probe, prop, tables, psi)
         halo_last(step, 1, first1)
-        middle(ext, offs, counts, measured, tables, psi, back, padded.at[1])
+        middle(ext, offs, counts, measured, tables, psi, back, wins, padded.at[1])
         sums1 = reduce_first(step, 1)
         backward_first(offs, probe, prop, tables, back, padded.at[0])
         reduce_second(step, 1, sums1)
@@ -468,6 +477,7 @@
                 pltpu.VMEM((2,) + field, F32),
                 pltpu.VMEM((SLOTS, 2) + field, F32),
                 pltpu.VMEM((SLOTS, 2) + field, F32),
+                pltpu.VMEM((SLOTS, 2) + field, F32),
                 pltpu.VMEM((2, SLOTS, 2, 2 * SIZE, SIZE), F32),
                 pltpu.SemaphoreType.DMA((ITERS, 2, COPIES)),
                 pltpu.SemaphoreType.DMA((ITERS, 2, COPIES)),

time: 77.7 us -> 70.3 us (0.905)
  Pallas kernels: 75.3 us -> 67.9 us
    pallas_call x1, Pallas kernels: 75.3 us -> 67.9 us  [on_device(): pl.pallas_call(functools.partial(kernel, shape), out_shape=jax.ShapeDtype...]
where the time goes in v2:
time: 70.3 us; the launch traced here: 70.1 us
  Pallas kernels  67.9 us (97%)
  local copies, waits for them, and re-layouts  1.57 us (2%)
    pallas_call x1, Pallas kernels, on_device(): pl.pallas_call(functools.partial(kernel, shape), out_shape=jax.ShapeDtype...  67.9 us
    unnamed x1, local copies, waits for them, and re-layouts  1.57 us

profile of v2, /device:TPU:8, one launch (start us, length us, event | category | flops | bytes accessed | tf_op | source)
XLA Modules:
  0.0 70.1 jit_solution(3019161574418636461)
XLA Ops:
  0.7 67.9 %shard_map.73 = f32[2,2,64,64]{3,2,1,0:T(8,128)} custom-call(f32[2,2,64,64]{3,2,1,0:T(8,128)} %obj_in.1, f32[2,128,128]{2,1,0:T(8,128)} %probe_in.1, f32[128,128]{1,0:T(8,128)} %phase_in.1, s32[1,1,2,6]{3,2,1,0:T(2,128)} %bitcast.1, s32[1,1]{1,0:T(1,128)S(6)} %copy.9.counts_in, f32[1,1,6,128,128]{4,3,2,1,0:T(8,128)} %measured_in.1, ...), custom_call_target="tpu_custom_call" | custom-call | tf_op jit(solution)/shard_map/pallas_call | solution.py:458
  68.6 1.6 %copy.10 = f32[2,2,64,64]{3,2,1,0:T(8,128)} copy(f32[2,2,64,64]{3,2,1,0:T(8,128)} %shard_map.73) | data formatting | bytes 131072

commit v3 on v2

--- a/solution.py
+++ b/solution.py
@@ -136,7 +136,7 @@
 PAIRS = tuple((2 * pair, 2 * pair + 1) for pair in range(SLOTS // 2))
 
 
-def forward_first(ext, offs, probe, prop, tables, psi):
+def forward_first(ext, offs, probe, prop, tables, psi, between):
     light = (probe[0], probe[1])
     fields = [
         times(light, load_window(ext, offs, 0, a)) + times(light, load_window(ext, offs, 0, b))
@@ -145,6 +145,7 @@
     fields = transform(fields, tables, FORWARD)
     factor = (prop[0], prop[1])
     fields = [times(field[:2], factor) + times(field[2:], factor) for field in fields]
+    between()
     fields = transform(fields, tables, INVERSE, True)
     for slots, field in zip(PAIRS, fields):
         for n, slot in enumerate(slots):
@@ -184,13 +185,14 @@
             )
 
 
-def backward_first(offs, probe, prop, tables, back, padded):
+def backward_first(offs, probe, prop, tables, back, padded, between):
     fields = [
         (back[a, 0], back[a, 1], back[b, 0], back[b, 1]) for a, b in PAIRS
     ]
     fields = transform(fields, tables, FORWARD)
     factor = (prop[0], prop[1])
     fields = [times_conj(field[:2], factor) + times_conj(field[2:], factor) for field in fields]
+    between()
     fields = transform(fields, tables, INVERSE, True)
     light = (probe[0], probe[1])
     for slots, field in zip(PAIRS, fields):
@@ -345,30 +347,34 @@
             tile(PAIR_DOWN, has_below),
         )
 
-    def reduce_first(step, s):
+    def reduce_rows(step, s, send_now):
         sent = grads.at[step, s]
-        copies = {}
-        for tile, kind, target in (
-            (ROW_UP, CORNER_DOWN, outer_above),
-            (ROW_DOWN, CORNER_UP, outer_below),
-            (ROW_OWN, ADD_OUT, outer),
-        ):
+        for tile in (ROW_UP, ROW_DOWN, ROW_OWN):
             first, second, third = gradient_rows(padded.at[s], offs, ROW_START[tile])
             sent[COL_OUT, tile] = jnp.where(even, first, third)
-            copies[kind] = send(
-                sent.at[COL_OUT, tile],
-                added.at[step, s, kind - 1],
+            sent[COL_PAIR, tile] = jnp.where(even, third, first)
+            sent[COL_OWN, tile] = second
+            send_now(tile)
+
+    def send_sum(step, s, kind, src, target):
+        return send(src, added.at[step, s, kind - 1], step, s, 8 + kind, target)
+
+    def reduce_first(step, s, copies, tile):
+        kind, target = {
+            ROW_UP: (CORNER_DOWN, outer_above),
+            ROW_DOWN: (CORNER_UP, outer_below),
+            ROW_OWN: (ADD_OUT, outer),
+        }[tile]
+        copies[kind] = send_sum(step, s, kind, grads.at[step, s, COL_OUT, tile], target)
+        if tile == ROW_OWN:
+            copies[ADD_PAIR] = send(
+                grads.at[step, s, COL_PAIR],
+                passed.at[step, s],
                 step,
                 s,
-                8 + kind,
-                target,
+                8 + ADD_PAIR,
+                partner,
             )
-            sent[COL_PAIR, tile] = jnp.where(even, third, first)
-            sent[COL_OWN, tile] = second
-        copies[ADD_PAIR] = send(
-            sent.at[COL_PAIR], passed.at[step, s], step, s, 8 + ADD_PAIR, partner
-        )
-        return copies
 
     def masked(step, s, kind, ok):
         return jnp.where(ok, added[step, s, kind - 1], 0.0)
@@ -378,14 +384,7 @@
         copies[ADD_PAIR].wait_recv()
         for tile, kind, target in ((ROW_UP, ADD_DOWN, above), (ROW_DOWN, ADD_UP, below)):
             mine[COL_OWN, tile] = mine[COL_OWN, tile] + passed[step, s, tile]
-            copies[kind] = send(
-                mine.at[COL_OWN, tile],
-                added.at[step, s, kind - 1],
-                step,
-                s,
-                8 + kind,
-                target,
-            )
+            copies[kind] = send_sum(step, s, kind, mine.at[COL_OWN, tile], target)
 
     def reduce_last(step, s, copies):
         total = grads[step, s, COL_OWN, ROW_OWN] + passed[step, s, ROW_OWN]
@@ -418,16 +417,30 @@
 
     for step in range(ITERS):
         halo_second(step, 0, first0)
-        halo_second(step, 1, first1)
         halo_last(step, 0, first0)
-        forward_first(ext, offs, probe, prop, tables, psi)
+        pass_halo = functools.partial(halo_second, step, 1, first1)
+        forward_first(ext, offs, probe, prop, tables, psi, pass_halo)
         halo_last(step, 1, first1)
         middle(ext, offs, counts, measured, tables, psi, back, wins, padded.at[1])
-        sums1 = reduce_first(step, 1)
-        backward_first(offs, probe, prop, tables, back, padded.at[0])
-        reduce_second(step, 1, sums1)
-        sums0 = reduce_first(step, 0)
+        sums0, sums1 = {}, {}
+        first_sums = functools.partial(reduce_first, step, 0, sums0)
+        last = step == ITERS - 1
+        if last:
+            reduce_rows(step, 1, functools.partial(reduce_first, step, 1, sums1))
+
+        def pass_sums():
+            if last:
+                reduce_second(step, 1, sums1)
+
+        backward_first(offs, probe, prop, tables, back, padded.at[0], pass_sums)
+        reduce_rows(step, 0, first_sums)
+        if not last:
+            reduce_rows(step, 1, lambda tile: None)
         reduce_second(step, 0, sums0)
+        if not last:
+            for tile in (ROW_UP, ROW_DOWN, ROW_OWN):
+                reduce_first(step, 1, sums1, tile)
+            reduce_second(step, 1, sums1)
         for s, sums in ((0, sums0), (1, sums1)):
             new = reduce_last(step, s, sums)
             if step < ITERS - 1:

time: 70.3 us -> 73.1 us (1.040)
  Pallas kernels: 67.9 us -> 70.7 us
    pallas_call x1, Pallas kernels: 67.9 us -> 70.7 us  [on_device(): pl.pallas_call(functools.partial(kernel, shape), out_shape=jax.ShapeDtype...]
where the time goes in v3:
time: 73.1 us; the launch traced here: 72.9 us
  Pallas kernels  70.7 us (97%)
  local copies, waits for them, and re-layouts  1.57 us (2%)
    pallas_call x1, Pallas kernels, on_device(): pl.pallas_call(functools.partial(kernel, shape), out_shape=jax.ShapeDtype...  70.7 us
    unnamed x1, local copies, waits for them, and re-layouts  1.57 us

profile of v3, /device:TPU:8, one launch (start us, length us, event | category | flops | bytes accessed | tf_op | source)
XLA Modules:
  0.0 72.9 jit_solution(6724267504166409740)
XLA Ops:
  0.7 70.7 %shard_map.73 = f32[2,2,64,64]{3,2,1,0:T(8,128)} custom-call(f32[2,2,64,64]{3,2,1,0:T(8,128)} %obj_in.1, f32[2,128,128]{2,1,0:T(8,128)} %probe_in.1, f32[128,128]{1,0:T(8,128)} %phase_in.1, s32[1,1,2,6]{3,2,1,0:T(2,128)} %bitcast.1, s32[1,1]{1,0:T(1,128)S(6)} %copy.9.counts_in, f32[1,1,6,128,128]{4,3,2,1,0:T(8,128)} %measured_in.1, ...), custom_call_target="tpu_custom_call" | custom-call | tf_op jit(solution)/shard_map/pallas_call | solution.py:471
  71.4 1.6 %copy.10 = f32[2,2,64,64]{3,2,1,0:T(8,128)} copy(f32[2,2,64,64]{3,2,1,0:T(8,128)} %shard_map.73) | data formatting | bytes 131072

commit v4 on v2

--- a/solution.py
+++ b/solution.py
@@ -21,8 +21,8 @@
 ROW_UP, ROW_DOWN, ROW_OWN = range(3)
 ROW_START = (0, 128, 64)
 COL_OUT, COL_OWN, COL_PAIR = range(3)
-ADD_PAIR, CORNER_UP, CORNER_DOWN, ADD_UP, ADD_DOWN, ADD_OUT = range(6)
-COPIES = 14
+ADD_PAIR, CORNER_UP, CORNER_DOWN, ADD_UP, ADD_DOWN, ADD_OUT, ADD_PAIR_OWN = range(7)
+COPIES = 15
 
 
 def dft_blocks():
@@ -300,11 +300,11 @@
         return {
             kind: send_halo(step, s, kind, mine, target)
             for kind, target in (
+                (DOWN, above),
+                (UP, below),
                 (OUT, outer),
                 (OUT_DOWN, outer_above),
                 (OUT_UP, outer_below),
-                (DOWN, above),
-                (UP, below),
                 (PAIR, partner),
             )
         }
@@ -345,6 +345,16 @@
             tile(PAIR_DOWN, has_below),
         )
 
+    def send_pair(step, s, copies, kind, tiles):
+        copies[kind] = send(
+            grads.at[step, s, COL_PAIR, tiles],
+            passed.at[step, s, tiles],
+            step,
+            s,
+            8 + kind,
+            partner,
+        )
+
     def reduce_first(step, s):
         sent = grads.at[step, s]
         copies = {}
@@ -354,6 +364,9 @@
             (ROW_OWN, ADD_OUT, outer),
         ):
             first, second, third = gradient_rows(padded.at[s], offs, ROW_START[tile])
+            sent[COL_PAIR, tile] = jnp.where(even, third, first)
+            if tile == ROW_DOWN:
+                send_pair(step, s, copies, ADD_PAIR, pl.ds(ROW_UP, 2))
             sent[COL_OUT, tile] = jnp.where(even, first, third)
             copies[kind] = send(
                 sent.at[COL_OUT, tile],
@@ -363,11 +376,8 @@
                 8 + kind,
                 target,
             )
-            sent[COL_PAIR, tile] = jnp.where(even, third, first)
             sent[COL_OWN, tile] = second
-        copies[ADD_PAIR] = send(
-            sent.at[COL_PAIR], passed.at[step, s], step, s, 8 + ADD_PAIR, partner
-        )
+        send_pair(step, s, copies, ADD_PAIR_OWN, pl.ds(ROW_OWN, 1))
         return copies
 
     def masked(step, s, kind, ok):
@@ -388,6 +398,7 @@
             )
 
     def reduce_last(step, s, copies):
+        copies[ADD_PAIR_OWN].wait_recv()
         total = grads[step, s, COL_OWN, ROW_OWN] + passed[step, s, ROW_OWN]
         both = jnp.logical_and
         for kind, ok in (

time: 70.3 us -> 69.5 us (0.989)
  Pallas kernels: 67.9 us -> 67.1 us
    pallas_call x1, Pallas kernels: 67.9 us -> 67.1 us  [on_device(): pl.pallas_call(functools.partial(kernel, shape), out_shape=jax.ShapeDtype...]
where the time goes in v4:
time: 69.5 us; the launch traced here: 69.3 us
  Pallas kernels  67.1 us (97%)
  local copies, waits for them, and re-layouts  1.57 us (2%)
    pallas_call x1, Pallas kernels, on_device(): pl.pallas_call(functools.partial(kernel, shape), out_shape=jax.ShapeDtype...  67.1 us
    unnamed x1, local copies, waits for them, and re-layouts  1.57 us

profile of v4, /device:TPU:8, one launch (start us, length us, event | category | flops | bytes accessed | tf_op | source)
XLA Modules:
  0.0 69.3 jit_solution(2955198509717916155)
XLA Ops:
  0.7 67.1 %shard_map.73 = f32[2,2,64,64]{3,2,1,0:T(8,128)} custom-call(f32[2,2,64,64]{3,2,1,0:T(8,128)} %obj_in.1, f32[2,128,128]{2,1,0:T(8,128)} %probe_in.1, f32[128,128]{1,0:T(8,128)} %phase_in.1, s32[1,1,2,6]{3,2,1,0:T(2,128)} %bitcast.1, s32[1,1]{1,0:T(1,128)S(6)} %copy.9.counts_in, f32[1,1,6,128,128]{4,3,2,1,0:T(8,128)} %measured_in.1, ...), custom_call_target="tpu_custom_call" | custom-call | tf_op jit(solution)/shard_map/pallas_call | solution.py:469
  67.8 1.6 %copy.10 = f32[2,2,64,64]{3,2,1,0:T(8,128)} copy(f32[2,2,64,64]{3,2,1,0:T(8,128)} %shard_map.73) | data formatting | bytes 131072

commit v5 on v4

--- a/solution.py
+++ b/solution.py
@@ -357,7 +357,7 @@
 
     def reduce_first(step, s):
         sent = grads.at[step, s]
-        copies = {}
+        copies, outward = {}, []
         for tile, kind, target in (
             (ROW_UP, CORNER_DOWN, outer_above),
             (ROW_DOWN, CORNER_UP, outer_below),
@@ -368,6 +368,9 @@
             if tile == ROW_DOWN:
                 send_pair(step, s, copies, ADD_PAIR, pl.ds(ROW_UP, 2))
             sent[COL_OUT, tile] = jnp.where(even, first, third)
+            outward.append((kind, tile, target))
+            sent[COL_OWN, tile] = second
+        for kind, tile, target in outward[::-1]:
             copies[kind] = send(
                 sent.at[COL_OUT, tile],
                 added.at[step, s, kind - 1],
@@ -376,7 +379,6 @@
                 8 + kind,
                 target,
             )
-            sent[COL_OWN, tile] = second
         send_pair(step, s, copies, ADD_PAIR_OWN, pl.ds(ROW_OWN, 1))
         return copies
 

time: 69.5 us -> 68.9 us (level)
  the two profiles are of different devices: /device:TPU:8 before, /device:TPU:1 now
where the time goes in v5:
time: 68.9 us; the launch traced here: 68.8 us
  Pallas kernels  66.5 us (97%)
  local copies, waits for them, and re-layouts  1.57 us (2%)
    pallas_call x1, Pallas kernels, on_device(): pl.pallas_call(functools.partial(kernel, shape), out_shape=jax.ShapeDtype...  66.5 us
    unnamed x1, local copies, waits for them, and re-layouts  1.57 us

profile of v5, /device:TPU:1, one launch (start us, length us, event | category | flops | bytes accessed | tf_op | source)
XLA Modules:
  0.0 68.8 jit_solution(15346312388489015247)
XLA Ops:
  0.7 66.5 %shard_map.73 = f32[2,2,64,64]{3,2,1,0:T(8,128)} custom-call(f32[2,2,64,64]{3,2,1,0:T(8,128)} %obj_in.1, f32[2,128,128]{2,1,0:T(8,128)} %probe_in.1, f32[128,128]{1,0:T(8,128)} %phase_in.1, s32[1,1,2,6]{3,2,1,0:T(2,128)} %bitcast.1, s32[1,1]{1,0:T(1,128)S(6)} %copy.9.counts_in, f32[1,1,6,128,128]{4,3,2,1,0:T(8,128)} %measured_in.1, ...), custom_call_target="tpu_custom_call" | custom-call | tf_op jit(solution)/shard_map/pallas_call | solution.py:471
  67.2 1.6 %copy.10 = f32[2,2,64,64]{3,2,1,0:T(8,128)} copy(f32[2,2,64,64]{3,2,1,0:T(8,128)} %shard_map.73) | data formatting | bytes 131072
